TPU v7x, 32 devices: a whole 2x2x4 slice. The times are simulated.
32 devices in a mesh: ch: 4 (over y, x), xy: 8 (over z, core).
Axes of the slice: x: 2, y: 2, z: 4, core: 2. Of those that a mesh axis runs over, the one named last changes fastest.
Arguments:
- inputs: bfloat16 [384, 1, 64, 128], P('ch', None, 'xy'), may hold values from -6 to 6
- weight: bfloat16 [9, 384, 384], P(None, 'ch'), may hold values from -0.125 to 0.125
- bias: float32 [384], P('ch'), may hold values from -3 to 3
- cotangent: bfloat16 [384, 1, 64, 128], P('ch', None, 'xy'), may hold values from -6 to 6
Outputs:
- output: bfloat16 [384, 1, 64, 128], P('ch', None, 'xy')
- grad_inputs: bfloat16 [384, 1, 64, 128], P('ch', None, 'xy')
- grad_weight: float32 [9, 384, 384], P(None, 'ch')
- grad_bias: float32 [384], P('ch')
All inputs are finite; a program needn't handle non-finite values.
Results may differ from a plain program's by a relative error of at most 0.0095.
Values may be sent and summed in bfloat16 or wider, within the bound.
A program may use at most 64 MiB of HBM per device.

v0:
```python
import jax
import jax.numpy as jnp
from jax import lax
from jax.sharding import PartitionSpec as P


def with_halo(shard, sides, width):
    for axis, dim in sides:
        devices, length = (lax.axis_size(axis), shard.shape[dim])
        up = [(i, (i + 1) % devices) for i in range(devices - 1)]
        down = [(j, i) for i, j in up]
        last = lax.slice_in_dim(shard, length - width, length, axis=dim)
        leading = lax.slice_in_dim(shard, 0, width, axis=dim)
        before = lax.ppermute(last, axis, up)
        after = lax.ppermute(leading, axis, down)
        shard = jnp.concatenate([before, shard, after], axis=dim)
    return shard


def tap_offsets():
    return [(a, b) for a in (-1, 0, 1) for b in (-1, 0, 1)]


def pad_columns(block):
    return jnp.pad(block, ((0, 0), (0, 0), (0, 0), (2, 2)))


def window_of(padded, a, b, rows, wide):
    count = padded.shape[0]
    return padded[:, :, 2 + 2 * a : 2 + 2 * a + rows, 2 + 2 * b : 2 + 2 * b + wide].reshape(
        count, -1
    )


def contract_lead(left, right):
    return lax.dot_general(
        left, right, (((0,), (0,)), ((), ())), preferred_element_type=jnp.float32
    )


def contract_last(left, right):
    return lax.dot_general(
        left, right, (((1,), (1,)), ((), ())), preferred_element_type=jnp.float32
    )


def activate(pre, cot_flat):
    output = jax.nn.gelu(pre, approximate=True).astype(jnp.bfloat16)
    _, pull = jax.vjp(lambda v: jax.nn.gelu(v, approximate=True), pre)
    grad_pre = pull(cot_flat.astype(jnp.float32))[0].astype(jnp.bfloat16)
    return (output, grad_pre)


def per_device(inputs, weight, bias, cotangent):
    chans, depth, rows, wide = inputs.shape
    out_local = bias.shape[0]
    cells = depth * rows * wide
    x_rim = with_halo(inputs, (("xy", 2),), 2)
    x_pad = pad_columns(x_rim)
    total = jnp.zeros((lax.axis_size("ch") * out_local, cells), jnp.float32)
    for t, (term_a, term_b) in enumerate(tap_offsets()):
        total = total + contract_lead(weight[t], window_of(x_pad, term_a, term_b, rows, wide))
    pre = lax.psum_scatter(
        total.reshape(lax.axis_size("ch") * out_local, depth, rows, wide),
        "ch",
        scatter_dimension=0,
        tiled=True,
    ).reshape(out_local, cells)
    pre = pre + bias[:, None]
    out_flat, grad_pre = activate(pre, cotangent.reshape(out_local, -1))
    g_rim = with_halo(grad_pre.reshape(out_local, depth, rows, wide), (("xy", 2),), 2)
    windows = [window_of(x_pad, a, b, rows, wide) for a, b in tap_offsets()]
    piece = lax.all_gather(g_rim, "ch", axis=0, tiled=True)
    grad_acc = jnp.zeros((chans, cells), jnp.float32)
    count = piece.shape[0]
    padded = pad_columns(piece)
    center = piece[:, :, 2 : 2 + rows, :].reshape(count, -1)
    pieces_w = []
    for t, (a, b) in enumerate(tap_offsets()):
        w_block = weight[t]
        g_win = padded[:, :, 2 - 2 * a : 2 - 2 * a + rows, 2 - 2 * b : 2 - 2 * b + wide].reshape(
            count, -1
        )
        grad_acc = grad_acc + jnp.dot(w_block, g_win, preferred_element_type=jnp.float32)
        pieces_w.append(contract_last(windows[t], center))
    fresh = jnp.stack(pieces_w, 0)
    grad_acc, grad_w = (grad_acc, fresh)
    grad_b = jnp.sum(grad_pre.astype(jnp.float32), axis=1)
    output = out_flat.reshape(out_local, depth, rows, wide)
    grad_x = grad_acc.astype(jnp.bfloat16).reshape(chans, depth, rows, wide)
    grad_w, grad_b = lax.psum((grad_w, grad_b), "xy")
    return (output, grad_x, grad_w, grad_b)


def solution(mesh):
    placed = (P("ch", None, "xy", None), P(None, "ch", None), P("ch"), P("ch", None, "xy", None))
    return jax.shard_map(
        per_device,
        mesh=mesh,
        in_specs=placed,
        out_specs=(
            P("ch", None, "xy", None),
            P("ch", None, "xy", None),
            P(None, "ch", None),
            P("ch"),
        ),
        check_vma=False,
    )
```

profile of v0, /device:TPU:0, one launch (start us, length us, event | category | flops | bytes accessed | tf_op | source)
XLA Modules:
  0.0 171.1 jit_solution(289212715683113014)
XLA Ops:
  8.2 2.4 %collective-permute-start = (bf16[96,1,2,128]{3,0,2,1:T(8,128)(2,1)S(1)}, bf16[96,1,2,128]{3,0,2,1:T(8,128)(2,1)S(1)}, u32[]{:S(2)}, u32[]{:S(2)}) collective-permute-start(bf16[96,1,2,128]{3,0,2,1:T(8,128)(2,1)S(1)} %get-tuple-element.34), channel_id=1, source_target_pairs={{0,1},{1,2},{2,3},{3,4},{4,5},{5,6},{6,7},{8,9},{9,10},{10,11},{11... | collective-permute-start | bytes 147464 | tf_op jit(solution)/shard_map/ppermute | solution.py:14
  10.6 1.3 collective-permute-start.1
  11.9 1.4 fusion.47
  13.2 2.6 %collective-permute-done.1 = bf16[96,1,2,128]{3,0,2,1:T(8,128)(2,1)S(1)} collective-permute-done((bf16[96,1,2,128]{3,0,2,1:T(8,128)(2,1)S(1)}, bf16[96,1,2,128]{3,0,2,1:T(8,128)(2,1)S(1)}, u32[]{:S(2)}, u32[]{:S(2)}) %collective-permute-start.1) | collective-permute-done | bytes 49184 | tf_op jit(solution)/shard_map/ppermute | solution.py:15
  21.8 1.6 copy.33
  23.5 33.7 %reduce-scatter.2.cloned.1.call-done = f32[96,1,8,128]{3,0,2,1:T(8,128)} async-done(((f32[384,1,8,128]{3,0,2,1:T(8,128)}), f32[96,1,8,128]{3,0,2,1:T(8,128)}) %reduce-scatter.2.cloned.1.call-update) | async-done | bytes 393232 | tf_op jit(solution)/shard_map/reduce_scatter | solution.py:63
  57.3 1.5 convert_reduce_fusion
  58.8 1.9 %collective-permute-start.2 = (bf16[96,1,2,128]{3,0,2,1:T(8,128)(2,1)S(1)}, bf16[96,1,2,128]{3,0,2,1:T(8,128)(2,1)S(1)}, u32[]{:S(2)}, u32[]{:S(2)}) collective-permute-start(bf16[96,1,2,128]{3,0,2,1:T(8,128)(2,1)S(1)} %get-tuple-element.30), channel_id=1, source_target_pairs={{0,1},{1,2},{2,3},{3,4},{4,5},{5,6},{6,7},{8,9},{9,10},{10,11},{11... | collective-permute-start | bytes 147464 | tf_op jit(solution)/shard_map/ppermute | solution.py:14
  60.7 1.3 collective-permute-start.3
  62.0 3.1 %collective-permute-done.3 = bf16[96,1,2,128]{3,0,2,1:T(8,128)(2,1)S(1)} collective-permute-done((bf16[96,1,2,128]{3,0,2,1:T(8,128)(2,1)S(1)}, bf16[96,1,2,128]{3,0,2,1:T(8,128)(2,1)S(1)}, u32[]{:S(2)}, u32[]{:S(2)}) %collective-permute-start.3) | collective-permute-done | bytes 49184 | tf_op jit(solution)/shard_map/ppermute | solution.py:15
  66.7 17.0 %psum.15 = f32[96]{0:T(128)} all-reduce(f32[96]{0:T(128)S(1)} %get-tuple-element.12), channel_id=1, replica_groups=mesh['ch'=4,'xy'=8] {'xy'}, use_global_device_ids=true, to_apply=%region_3.4 | all-reduce | flops 96 | bytes 768 | tf_op jit(solution)/shard_map/psum | solution.py:91
  83.7 11.5 %all-gather.2.cloned.1.call-done = bf16[384,1,12,128]{3,0,2,1:T(8,128)(2,1)} async-done(((bf16[96,1,12,128]{3,0,2,1:T(8,128)(2,1)}), bf16[384,1,12,128]{3,0,2,1:T(8,128)(2,1)}) %all-gather.2.cloned.1.call-update) | async-done | bytes 1179664 | tf_op jit(solution)/shard_map/all_gather | solution.py:73
  95.2 1.6 fusion.11
  96.8 1.5 fusion.10
  102.4 3.1 %pad_slice_fusion = (bf16[384,1,8,128]{3,0,2,1:T(8,128)(2,1)}, bf16[384,1,8,128]{3,0,2,1:T(8,128)(2,1)}, bf16[384,1,8,128]{3,0,2,1:T(8,128)(2,1)S(1)}, bf16[384,...) fusion(bf16[384,1,12,128]{3,0,2,1:T(8,128)(2,1)S(1)} %copy-done), kind=kLoop, calls=%fused_computation | loop fusion | bytes 10616832 | tf_op jit(solution)/shard_map/slice | solution.py:81
  105.5 1.6 copy.43
  110.2 1.5 copy.42
  111.7 2.3 %copy.39 = bf16[384,1,8,128]{0,3,2,1:T(8,128)(2,1)} copy(bf16[384,1,8,128]{3,0,2,1:T(8,128)(2,1)} %get-tuple-element.20) | data formatting | bytes 1572864 | tf_op jit(solution)/shard_map/slice | solution.py:81
  114.0 2.3 %copy.36 = bf16[384,1,8,128]{0,3,2,1:T(8,128)(2,1)} copy(bf16[384,1,8,128]{3,0,2,1:T(8,128)(2,1)} %get-tuple-element.21) | data formatting | bytes 1572864 | tf_op jit(solution)/shard_map/slice | solution.py:81
  116.3 2.3 %copy.35 = bf16[384,1,8,128]{0,3,2,1:T(8,128)(2,1)} copy(bf16[384,1,8,128]{3,0,2,1:T(8,128)(2,1)} %get-tuple-element.22) | data formatting | bytes 1572864 | tf_op jit(solution)/shard_map/slice | solution.py:81
  118.6 1.7 fusion.87
  120.3 1.3 convolution_add_fusion.7
  125.4 36.7 %all-reduce.4.cloned.1.call-done = f32[9,96,384]{2,1,0:T(8,128)} async-done(((f32[9,96,384]{2,1,0:T(8,128)}), f32[9,96,384]{2,1,0:T(8,128)}) %all-reduce.4.cloned.1.call-update) | async-done | bytes 1327120 | tf_op jit(solution)/shard_map/psum | solution.py:91
  162.1 2.5 %copy.107 = f32[9,96,384]{2,1,0:T(8,128)} copy(f32[9,96,384]{2,1,0:T(8,128)} %all-reduce.4.cloned.1.call-done) | data formatting | bytes 2654208
  (85 shorter events, 19.3 us)
Async XLA Ops:
  7.2 50.1 %reduce-scatter.2.cloned.1.call-start = ((), (), s32[]{:S(2)}) async-start(), calls=%async_computation.1 | async-start | bytes 1966080 | tf_op jit(solution)/shard_map/reduce_scatter | solution.py:63
  8.2 5.0 %collective-permute-start = (bf16[96,1,2,128]{3,0,2,1:T(8,128)(2,1)S(1)}, bf16[96,1,2,128]{3,0,2,1:T(8,128)(2,1)S(1)}, u32[]{:S(2)}, u32[]{:S(2)}) collective-permute-start(bf16[96,1,2,128]{3,0,2,1:T(8,128)(2,1)S(1)} %get-tuple-element.34), channel_id=1, source_target_pairs={{0,1},{1,2},{2,3},{3,4},{4,5},{5,6},{6,7},{8,9},{9,10},{10,11},{11... | collective-permute-start | bytes 147464 | tf_op jit(solution)/shard_map/ppermute | solution.py:14
  10.6 5.3 %collective-permute-start.1 = (bf16[96,1,2,128]{3,0,2,1:T(8,128)(2,1)S(1)}, bf16[96,1,2,128]{3,0,2,1:T(8,128)(2,1)S(1)}, u32[]{:S(2)}, u32[]{:S(2)}) collective-permute-start(bf16[96,1,2,128]{3,0,2,1:T(8,128)(2,1)S(1)} %get-tuple-element.35), channel_id=1, source_target_pairs={{1,0},{2,1},{3,2},{4,3},{5,4},{6,5},{7,6},{9,8},{10,9},{11,10},{12... | collective-permute-start | bytes 147464 | tf_op jit(solution)/shard_map/ppermute | solution.py:15
  15.9 0.7 copy-start.11
  15.9 0.7 copy-start.13
  17.2 1.1 copy-start.7
  23.5 33.8 %copy-start.15 = (bf16[96,1,8,128]{3,2,1,0:T(8,128)(2,1)S(1)}, bf16[96,1,8,128]{3,2,1,0:T(8,128)(2,1)}, u32[]{:S(2)}) copy-start(bf16[96,1,8,128]{3,2,1,0:T(8,128)(2,1)} %param.7) | copy-start | bytes 589828
  23.5 33.8 %copy-start.16 = (f32[96]{0:T(128)S(1)}, f32[96]{0:T(128)}, u32[]{:S(2)}) copy-start(f32[96]{0:T(128)} %param.6) | copy-start | bytes 1156
  23.5 71.7 %all-gather.2.cloned.1.call-start = ((), (), s32[]{:S(2)}) async-start(), calls=%async_computation.2 | async-start | bytes 1474560 | tf_op jit(solution)/shard_map/all_gather | solution.py:73
  58.8 38.1 %copy-start.14 = (bf16[96,1,8,128]{3,0,2,1:T(8,128)(2,1)S(1)}, bf16[96,1,8,128]{3,0,2,1:T(8,128)(2,1)}, u32[]{:S(2)}) copy-start(bf16[96,1,8,128]{3,0,2,1:T(8,128)(2,1)} %copy-done.13) | copy-start | bytes 589828
  58.8 3.2 %collective-permute-start.2 = (bf16[96,1,2,128]{3,0,2,1:T(8,128)(2,1)S(1)}, bf16[96,1,2,128]{3,0,2,1:T(8,128)(2,1)S(1)}, u32[]{:S(2)}, u32[]{:S(2)}) collective-permute-start(bf16[96,1,2,128]{3,0,2,1:T(8,128)(2,1)S(1)} %get-tuple-element.30), channel_id=1, source_target_pairs={{0,1},{1,2},{2,3},{3,4},{4,5},{5,6},{6,7},{8,9},{9,10},{10,11},{11... | collective-permute-start | bytes 147464 | tf_op jit(solution)/shard_map/ppermute | solution.py:14
  60.7 4.4 %collective-permute-start.3 = (bf16[96,1,2,128]{3,0,2,1:T(8,128)(2,1)S(1)}, bf16[96,1,2,128]{3,0,2,1:T(8,128)(2,1)S(1)}, u32[]{:S(2)}, u32[]{:S(2)}) collective-permute-start(bf16[96,1,2,128]{3,0,2,1:T(8,128)(2,1)S(1)} %get-tuple-element.31), channel_id=1, source_target_pairs={{1,0},{2,1},{3,2},{4,3},{5,4},{6,5},{7,6},{9,8},{10,9},{11,10},{12... | collective-permute-start | bytes 147464 | tf_op jit(solution)/shard_map/ppermute | solution.py:15
  65.9 96.2 %all-reduce.4.cloned.1.call-start = ((), (), s32[]{:S(2)}) async-start(), calls=%async_computation.3 | async-start | bytes 2654208 | tf_op jit(solution)/shard_map/psum | solution.py:91
  95.2 3.1 %copy-start = (bf16[384,1,12,128]{3,0,2,1:T(8,128)(2,1)S(1)}, bf16[384,1,12,128]{3,0,2,1:T(8,128)(2,1)}, u32[]{:S(2)}) copy-start(bf16[384,1,12,128]{3,0,2,1:T(8,128)(2,1)} %all-gather.2.cloned.1.call-done) | copy-start | bytes 3538948
  98.3 0.9 copy-start.10
  99.6 0.9 copy-start.12
  101.3 1.1 copy-start.9
  105.5 1.6 copy-start.6
  108.3 1.5 copy-start.5
  118.6 1.7 copy-start.4
  118.6 3.0 %copy-start.2 = (bf16[384,1,8,128]{0,3,2,1:T(8,128)(2,1)S(1)}, bf16[384,1,8,128]{0,3,2,1:T(8,128)(2,1)}, u32[]{:S(2)}) copy-start(bf16[384,1,8,128]{0,3,2,1:T(8,128)(2,1)} %copy.37) | copy-start | bytes 2359300
  118.6 3.0 %copy-start.8 = (bf16[9,96,384]{2,1,0:T(8,128)(2,1)S(1)}, bf16[9,96,384]{2,1,0:T(8,128)(2,1)}, u32[]{:S(2)}) copy-start(bf16[9,96,384]{2,1,0:T(8,128)(2,1)} %param.5) | copy-start | bytes 1990660
  120.3 1.7 %copy-start.1 = (bf16[384,1,8,128]{0,3,2,1:T(8,128)(2,1)S(1)}, bf16[384,1,8,128]{0,3,2,1:T(8,128)(2,1)}, u32[]{:S(2)}) copy-start(bf16[384,1,8,128]{0,3,2,1:T(8,128)(2,1)} %copy.38) | copy-start | bytes 2359300
  121.7 1.1 copy-start.3
Sparse Core Ops, SparseCore 0:
  23.6 33.5 reduce-scatter.1
  66.0 29.2 all-gather.1
  102.5 59.5 all-reduce.3
where the time goes:
time: 172 us; the launch traced here: 171 us
  waiting for transfers between devices  87.7 us (51%)
  local copies, waits for them, and re-layouts  26.6 us (15%)
  blocking collectives  17 us (10%)
  matrix products  16.2 us (9%)
  between operations  14.1 us (8%)
  starting transfers between devices  6.94 us (4%)
  other arithmetic  2.55 us (1%)
    psum x1, waiting for transfers between devices, per_device(): grad_w, grad_b = lax.psum((grad_w, grad_b), 'xy')  36.7 us
    reduce_scatter x1, waiting for transfers between devices, per_device(): lax.psum_scatter(total.reshape(lax.axis_size('ch') * out_local, depth, ro...  33.7 us
    psum x1, blocking collectives, per_device(): grad_w, grad_b = lax.psum((grad_w, grad_b), 'xy')  17 us
    slice x10, local copies, waits for them, and re-layouts, per_device(): padded[:, :, 2 - 2 * a:2 - 2 * a + rows, 2 - 2 * b:2 - 2 * b + wide]  16.2 us
    all_gather x1, waiting for transfers between devices, per_device(): piece = lax.all_gather(g_rim, 'ch', axis=0, tiled=True)  11.5 us
    unnamed x38, local copies, waits for them, and re-layouts  7.86 us
    ppermute x2, waiting for transfers between devices, with_halo(): after = lax.ppermute(leading, axis, down)  5.72 us
    dot_general x9, matrix products, contract_last(): lax.dot_general(left, right, (((1,), (1,)), ((), ())), preferred_element_...  5.65 us
  transfers between devices with their start and end apart: 7, of which 5 were waited for; matrix products, arithmetic and copies ran while one was open for 14% of the time, Pallas kernels for 0%

commit v1 on v0

--- a/solution.py
+++ b/solution.py
@@ -1,6 +1,11 @@
+import functools
+import math
+
 import jax
 import jax.numpy as jnp
 from jax import lax
+from jax.experimental import pallas as pl
+from jax.experimental.pallas import tpu as pltpu
 from jax.sharding import PartitionSpec as P
 
 
@@ -92,10 +97,338 @@
     return (output, grad_x, grad_w, grad_b)
 
 
+F32 = jnp.float32
+BF16 = jnp.bfloat16
+SLOPE = math.sqrt(2.0 / math.pi)
+
+
+def fused_kernel(
+    nch, nxy, x_ref, w_ref, b_ref, cot_ref,
+    out_ref, gx_ref, gw_ref, gb_ref,
+    xrow, crow, orow, x2d, xim, pf, pb, prv, g2d, sacc,
+    gwf, csend, crecv, zsend, zrecv, fin,
+    xs, xr, ps, pr, gs, gr, hs, hr, cs, cr, zs, zr, as_, ar, fs, fr,
+):
+    cl, rows, wide = x_ref.shape
+    co = w_ref.shape[1]
+    cells = rows * wide
+    rim = 2 * wide
+    half = cells // 2
+    kc = 9 * cl
+    me = lax.axis_index("ch")
+    xy = lax.axis_index("xy")
+    core = lax.rem(xy, 2)
+    nz = nxy // 2
+    z = xy // 2
+    hr_rows = crecv.shape[0]
+    shard = hr_rows // nz
+    part = kc // 2
+
+    def peer(d):
+        return lax.rem(me + d, nch)
+
+    def zpeer(d):
+        return lax.rem(z + d, nz) * 2 + core
+
+    def remote(src, dst, ssem, rsem, **where):
+        return pltpu.make_async_remote_copy(
+            src_ref=src, dst_ref=dst, send_sem=ssem, recv_sem=rsem,
+            device_id=where, device_id_type=pl.DeviceIdType.MESH,
+        )
+
+    barrier = pltpu.get_barrier_semaphore()
+    for d in range(1, nch):
+        pl.semaphore_signal(barrier, inc=1, device_id={"ch": peer(d)}, device_id_type=pl.DeviceIdType.MESH)
+    for d in range(1, nxy):
+        pl.semaphore_signal(
+            barrier, inc=1, device_id={"xy": lax.rem(xy + d, nxy)}, device_id_type=pl.DeviceIdType.MESH
+        )
+
+    up = xy > 0
+    down = xy < nxy - 1
+
+    xrow[...] = x_ref[...].astype(F32).reshape(cl * rows, wide)
+    crow[...] = cot_ref[...].astype(F32).reshape(cl * rows, wide)
+    for r in range(rows):
+        x2d[:, rim + r * wide : rim + (r + 1) * wide] = xrow[pl.ds(r, cl, stride=rows), :].astype(BF16)
+
+    pl.semaphore_wait(barrier, nch - 1 + nxy - 1)
+
+    to_up = remote(x2d.at[:, pl.ds(rim, rim)], x2d.at[:, pl.ds(rim + cells, rim)], xs.at[0], xr.at[0], xy=jnp.maximum(xy - 1, 0))
+    to_down = remote(x2d.at[:, pl.ds(cells, rim)], x2d.at[:, pl.ds(0, rim)], xs.at[1], xr.at[1], xy=jnp.minimum(xy + 1, nxy - 1))
+    pl.when(up)(to_up.start)
+    pl.when(down)(to_down.start)
+
+    lane = lax.broadcasted_iota(jnp.int32, (cl, wide), 1)
+
+    def spread(src_row):
+        v = x2d[:, src_row * wide : (src_row + 1) * wide]
+        vf = v.astype(F32)
+        minus = jnp.where(lane >= 2, pltpu.roll(vf, 2, 1), 0.0).astype(BF16)
+        plus = jnp.where(lane < wide - 2, pltpu.roll(vf, wide - 2, 1), 0.0).astype(BF16)
+        for a in (-1, 0, 1):
+            r = src_row - 2 - 2 * a
+            if 0 <= r < rows:
+                for b, val in ((-1, minus), (0, v), (1, plus)):
+                    t = 3 * (a + 1) + b + 1
+                    xim[t * cl : (t + 1) * cl, r * wide : (r + 1) * wide] = val
+
+    for src_row in range(2, rows + 2):
+        spread(src_row)
+    xim[kc:, :] = jnp.ones((xim.shape[0] - kc, cells), BF16)
+
+    def edge_zero(cond, ref, start):
+        @pl.when(jnp.logical_not(cond))
+        def _():
+            ref[:, start : start + rim] = jnp.zeros((ref.shape[0], rim), BF16)
+
+    edge_zero(up, x2d, 0)
+    edge_zero(down, x2d, rim + cells)
+    edge_zero(up, g2d, 0)
+    edge_zero(down, g2d, rim + cells)
+
+    eye = lax.broadcasted_iota(jnp.int32, (cl, cl), 0) == lax.broadcasted_iota(jnp.int32, (cl, cl), 1)
+    bias = jnp.sum(jnp.where(eye, jnp.broadcast_to(b_ref[...], (cl, cl)), 0.0), axis=1, keepdims=True)
+
+    pl.when(up)(to_down.wait_recv)
+    pl.when(down)(to_up.wait_recv)
+    for src_row in (0, 1, rows + 2, rows + 3):
+        spread(src_row)
+
+    own = pl.ds(pl.multiple_of(me * cl, 16), cl)
+    psends = []
+    for h in range(2):
+        cols = pl.ds(h * half, half)
+        val = contract_lead(w_ref[...], xim[:kc, h * half : (h + 1) * half])
+        pf[:, cols] = val
+        pb[:, cols] = val.astype(BF16)
+        for d in range(1, nch):
+            there = pl.ds(pl.multiple_of(peer(d) * cl, 16), cl)
+            k = h * (nch - 1) + d - 1
+            c = remote(pb.at[there, cols], prv.at[d - 1, :, cols], ps.at[k], pr.at[k], ch=peer(d))
+            c.start()
+            psends.append(c)
+
+    gsends = []
+    hsends = {}
+
+    def halo_sends(d, which):
+        blk = pl.ds(pl.multiple_of(lax.rem(me - d + nch, nch) * cl, 16), cl)
+        if which == 0:
+            c = remote(
+                g2d.at[blk, pl.ds(rim, rim)], g2d.at[blk, pl.ds(rim + cells, rim)],
+                hs.at[d], hr.at[d], xy=jnp.maximum(xy - 1, 0),
+            )
+            pl.when(up)(c.start)
+        else:
+            c = remote(
+                g2d.at[blk, pl.ds(cells, rim)], g2d.at[blk, pl.ds(0, rim)],
+                hs.at[nch + d], hr.at[nch + d], xy=jnp.minimum(xy + 1, nxy - 1),
+            )
+            pl.when(down)(c.start)
+        hsends[(d, which)] = c
+
+    for h in range(2):
+        cols = pl.ds(h * half, half)
+        for d in range(1, nch):
+            psends[h * (nch - 1) + d - 1].wait_recv()
+        for r in range(h * rows // 2, (h + 1) * rows // 2):
+            rc = pl.ds(r * wide, wide)
+            v = pf[own, rc] + bias
+            for d in range(1, nch):
+                v = v + prv[d - 1, :, rc].astype(F32)
+            sq = v * v
+            th = jnp.tanh(SLOPE * (v + 0.044715 * (sq * v)))
+            hp = 0.5 * (1.0 + th)
+            orow[pl.ds(r, cl, stride=rows), :] = v * hp
+            slope = hp + 0.5 * v * (1.0 - th * th) * (SLOPE * (1.0 + 3.0 * 0.044715 * sq))
+            g = crow[pl.ds(r, cl, stride=rows), :] * slope
+            g2d[own, pl.ds(rim + r * wide, wide)] = g.astype(BF16)
+        for d in range(1, nch):
+            k = h * (nch - 1) + d - 1
+            blk = g2d.at[own, pl.ds(rim + h * half, half)]
+            c = remote(blk, blk, gs.at[k], gr.at[k], ch=peer(d))
+            c.start()
+            gsends.append(c)
+        halo_sends(0, h)
+
+    out_ref[...] = orow[...].reshape(cl, rows, wide).astype(BF16)
+
+    for h in range(2):
+        for d in range(1, nch):
+            gsends[h * (nch - 1) + d - 1].wait_recv()
+            halo_sends(d, h)
+
+    gwf[...] = contract_last(xim[...], g2d[:, rim : rim + cells])
+    theirs = pl.ds(pl.multiple_of((1 - core) * part, 16), hr_rows)
+    mine = pl.ds(pl.multiple_of(core * part, 16), hr_rows)
+    csend[...] = gwf[theirs, :].astype(BF16)
+    partner = xy + 1 - 2 * core
+    ccopy = remote(csend, crecv, cs.at[0], cr.at[0], xy=partner)
+    ccopy.start()
+
+    for d in range(nch):
+        pl.when(up)(hsends[(d, 1)].wait_recv)
+        pl.when(down)(hsends[(d, 0)].wait_recv)
+
+    pairs = rows // 2
+    group = 3 * cl
+
+    def gi_chunk(k, first):
+        val = jnp.dot(w_ref[...], g2d[:, k * rim : (k + 1) * rim], preferred_element_type=F32)
+        for a in (-1, 0, 1):
+            q = k - 1 + a
+            if 0 <= q < pairs:
+                piece = val[(a + 1) * group : (a + 2) * group]
+                if q in first:
+                    sacc[:, q * rim : (q + 1) * rim] += piece
+                else:
+                    first.add(q)
+                    sacc[:, q * rim : (q + 1) * rim] = piece
+
+    seen = set()
+    for k in range(2):
+        gi_chunk(k, seen)
+
+    ccopy.wait_recv()
+    mysum = gwf[mine, :] + crecv[...].astype(F32)
+    gwf[mine, :] = mysum
+    zsend[...] = mysum.astype(BF16)
+    zcopies = []
+    for d in range(1, nz):
+        at = pl.ds(pl.multiple_of(lax.rem(z + d, nz) * shard, 16), shard)
+        c = remote(zsend.at[at, :], zrecv.at[d - 1], zs.at[d - 1], zr.at[d - 1], xy=zpeer(d))
+        c.start()
+        zcopies.append(c)
+
+    for k in range(2, pairs + 2):
+        gi_chunk(k, seen)
+    for r in range(rows):
+        rc = slice(r * wide, (r + 1) * wide)
+        v = sacc[cl : 2 * cl, rc]
+        v = v + jnp.where(lane < wide - 2, pltpu.roll(sacc[:cl, rc], wide - 2, 1), 0.0)
+        v = v + jnp.where(lane >= 2, pltpu.roll(sacc[2 * cl :, rc], 2, 1), 0.0)
+        xrow[pl.ds(r, cl, stride=rows), :] = v
+    gx_ref[...] = xrow[...].reshape(cl, rows, wide).astype(BF16)
+
+    for c in zcopies:
+        c.wait_recv()
+    total = gwf[pl.ds(pl.multiple_of(core * part + z * shard, 16), shard), :]
+    for d in range(1, nz):
+        total = total + zrecv[d - 1].astype(F32)
+    sh = pl.ds(pl.multiple_of(z * shard, 16), shard)
+    fin[core, sh, :] = total.astype(BF16)
+    acopies = []
+    fcopies = []
+    blk = fin.at[core, sh, :]
+    fcopies.append(remote(blk, blk, fs.at[0], fr.at[0], xy=partner))
+    for d in range(1, nz):
+        c = remote(blk, blk, as_.at[d - 1], ar.at[d - 1], xy=zpeer(d))
+        c.start()
+        acopies.append(c)
+    fcopies[0].start()
+    for d in range(1, nz):
+        acopies[d - 1].wait_recv()
+        src = pl.ds(pl.multiple_of(lax.rem(z - d + nz, nz) * shard, 16), shard)
+        blk = fin.at[core, src, :]
+        c = remote(blk, blk, fs.at[d], fr.at[d], xy=partner)
+        c.start()
+        fcopies.append(c)
+    for c in fcopies:
+        c.wait_recv()
+    gw_ref[:part, :] = fin[0, :part, :].astype(F32)
+    gw_ref[part:, :] = fin[1, :part, :].astype(F32)
+    pick = (
+        lax.broadcasted_iota(jnp.int32, (co, wide), 0) == lax.broadcasted_iota(jnp.int32, (co, wide), 1) + me * cl
+    ).astype(F32).astype(BF16)
+    gb = jnp.dot(fin[1, part:, :], pick, preferred_element_type=F32)
+    gb_ref[...] = gb[0:1, :cl]
+
+    pl.when(up)(to_up.wait_send)
+    pl.when(down)(to_down.wait_send)
+    for c in psends + gsends + zcopies + acopies + fcopies + [ccopy]:
+        c.wait_send()
+    for d in range(nch):
+        pl.when(up)(hsends[(d, 0)].wait_send)
+        pl.when(down)(hsends[(d, 1)].wait_send)
+
+
+def fits(chans, depth, rows, wide, nxy):
+    part = 9 * chans // 2
+    return (
+        depth == 1
+        and rows % 4 == 0
+        and wide == 128
+        and chans % 32 == 0
+        and chans <= wide
+        and nxy % 2 == 0
+        and (part + 16) % (16 * (nxy // 2)) == 0
+    )
+
+
+def layer(inputs, weight, bias, cotangent):
+    chans, depth, rows, wide = inputs.shape
+    nch, nxy = lax.axis_size("ch"), lax.axis_size("xy")
+    if not fits(chans, depth, rows, wide, nxy):
+        return per_device(inputs, weight, bias, cotangent)
+    co = weight.shape[2]
+    cells = rows * wide
+    kc = 9 * chans
+    nz = nxy // 2
+    hrows = kc // 2 + 16
+    dma = pltpu.SemaphoreType.DMA
+    vmem = pltpu.VMEM
+    sems = [2, 2] + [2 * (nch - 1)] * 4 + [2 * nch] * 2 + [1, 1] + [nz - 1] * 4 + [nz, nz]
+    out, gx, gw, gb = pl.pallas_call(
+        functools.partial(fused_kernel, nch, nxy),
+        out_shape=(
+            jax.ShapeDtypeStruct((chans, rows, wide), BF16),
+            jax.ShapeDtypeStruct((chans, rows, wide), BF16),
+            jax.ShapeDtypeStruct((kc, co), F32),
+            jax.ShapeDtypeStruct((1, chans), F32),
+        ),
+        in_specs=[pl.BlockSpec(memory_space=vmem)] * 4,
+        out_specs=[pl.BlockSpec(memory_space=vmem)] * 4,
+        scratch_shapes=[
+            vmem((chans * rows, wide), F32),
+            vmem((chans * rows, wide), F32),
+            vmem((chans * rows, wide), F32),
+            vmem((chans, cells + 4 * wide), BF16),
+            vmem((kc + 16, cells), BF16),
+            vmem((co, cells), F32),
+            vmem((co, cells), BF16),
+            vmem((nch - 1, chans, cells), BF16),
+            vmem((co, cells + 4 * wide), BF16),
+            vmem((3 * chans, cells), F32),
+            vmem((kc + 16, co), F32),
+            vmem((hrows, co), BF16),
+            vmem((hrows, co), BF16),
+            vmem((hrows, co), BF16),
+            vmem((nz - 1, hrows // nz, co), BF16),
+            vmem((2, hrows, co), BF16),
+        ]
+        + [dma((n,)) for n in sems],
+        compiler_params=pltpu.CompilerParams(
+            collective_id=0, has_side_effects=True, vmem_limit_bytes=48 * 1024 * 1024
+        ),
+    )(
+        inputs.reshape(chans, rows, wide),
+        weight.reshape(kc, co),
+        bias.reshape(1, chans),
+        cotangent.reshape(chans, rows, wide),
+    )
+    return (
+        out.reshape(chans, depth, rows, wide),
+        gx.reshape(chans, depth, rows, wide),
+        gw.reshape(9, chans, co),
+        gb.reshape(chans),
+    )
+
+
 def solution(mesh):
     placed = (P("ch", None, "xy", None), P(None, "ch", None), P("ch"), P("ch", None, "xy", None))
     return jax.shard_map(
-        per_device,
+        layer,
         mesh=mesh,
         in_specs=placed,
         out_specs=(

time: 172 us -> 56 us (0.33)
  waiting for transfers between devices: 87.7 us -> 0 us
  Pallas kernels: 0 us -> 48 us
  local copies, waits for them, and re-layouts: 26.6 us -> 6.52 us
  blocking collectives: 17 us -> 0 us
  matrix products: 16.2 us -> 0 us
  between operations: 14.1 us -> 0.65 us
  starting transfers between devices: 6.94 us -> 0 us
  other arithmetic: 2.55 us -> 0 us
    pallas_call x0 -> x1, Pallas kernels: none -> 48 us  [layer(): pl.pallas_call(functools.partial(fused_kernel, nch, nxy), out_shape=(jax....]
    psum x1 -> x0, waiting for transfers between devices: 36.7 us -> none  [per_device(): grad_w, grad_b = lax.psum((grad_w, grad_b), 'xy')]
    reduce_scatter x1 -> x0, waiting for transfers between devices: 33.7 us -> none  [per_device(): lax.psum_scatter(total.reshape(lax.axis_size('ch') * out_local, depth, ro...]
    slice x21 -> x0, local copies, waits for them, and re-layouts: 17.1 us -> none  [the longest x10 16.2 us: per_device(): padded[:, :, 2 - 2 * a:2 - 2 * a + rows, 2 - 2 * b:2 - 2 * b + wide]]
    psum x1 -> x0, blocking collectives: 17 us -> none  [per_device(): grad_w, grad_b = lax.psum((grad_w, grad_b), 'xy')]
    dot_general x27 -> x0, matrix products: 16.2 us -> none  [the longest x9 5.65 us: contract_last(): lax.dot_general(left, right, (((1,), (1,)), ((), ())), preferred_element_...]
    all_gather x1 -> x0, waiting for transfers between devices: 11.5 us -> none  [per_device(): piece = lax.all_gather(g_rim, 'ch', axis=0, tiled=True)]
    ppermute x4 -> x0, starting transfers between devices: 6.82 us -> none  [the longest x2 4.24 us: with_halo(): before = lax.ppermute(last, axis, up)]
  transfers between devices with their start and end apart: 7 -> 0, of which waited for: 5 -> 0; matrix products, arithmetic and copies ran while one was open for 14% -> 0% of each run, Pallas kernels for 0% -> 0%
where the time goes in v1:
time: 56 us; the launch traced here: 55.2 us
  Pallas kernels  48 us (86%)
  local copies, waits for them, and re-layouts  6.52 us (12%)
  between operations  0.65 us (1%)
    pallas_call x1, Pallas kernels, layer(): pl.pallas_call(functools.partial(fused_kernel, nch, nxy), out_shape=(jax....  48 us
    unnamed x12, local copies, waits for them, and re-layouts  6.52 us

profile of v1, /device:TPU:0, one launch (start us, length us, event | category | flops | bytes accessed | tf_op | source)
XLA Modules:
  0.0 55.2 jit_solution(14800119986321155696)
XLA Ops:
  0.6 0.0 copy-start
  0.6 1.1 %copy-done = bf16[9,96,384]{2,1,0:T(8,128)(2,1)S(1)} copy-done((bf16[9,96,384]{2,1,0:T(8,128)(2,1)S(1)}, bf16[9,96,384]{2,1,0:T(8,128)(2,1)}, u32[]{:S(2)}) %copy-start) | copy-done | bytes 663576
  1.7 0.0 copy-start.1
  1.7 0.9 %copy-done.1 = bf16[96,1,8,128]{3,2,1,0:T(8,128)(2,1)S(1)} copy-done((bf16[96,1,8,128]{3,2,1,0:T(8,128)(2,1)S(1)}, bf16[96,1,8,128]{3,2,1,0:T(8,128)(2,1)}, u32[]{:S(2)}) %copy-start.1) | copy-done | bytes 196632
  2.6 0.0 copy-start.2
  2.7 0.9 %copy-done.2 = bf16[96,1,8,128]{3,2,1,0:T(8,128)(2,1)S(1)} copy-done((bf16[96,1,8,128]{3,2,1,0:T(8,128)(2,1)S(1)}, bf16[96,1,8,128]{3,2,1,0:T(8,128)(2,1)}, u32[]{:S(2)}) %copy-start.2) | copy-done | bytes 196632
  3.6 0.0 copy-start.3
  3.6 0.7 %copy-done.3 = f32[96]{0:T(128)S(1)} copy-done((f32[96]{0:T(128)S(1)}, f32[96]{0:T(128)}, u32[]{:S(2)}) %copy-start.3) | copy-done | bytes 408
  4.2 48.0 %shard_map.75 = (bf16[96,8,128]{2,1,0:T(8,128)(2,1)S(1)}, bf16[96,8,128]{2,1,0:T(8,128)(2,1)S(1)}, f32[864,384]{1,0:T(8,128)S(1)}, f32[1,96]{1,0:T(1,128)S(1)}) custom-call(bf16[96,8,128]{2,1,0:T(8,128)(2,1)S(1)} %bitcast.16, bf16[864,384]{1,0:T(8,128)(2,1)S(1)} %bitcast.13, f32[1,96]{1,0:T(1,128)S(1)} %bitcast.18, bf16[96,8,128]{2,1,0:T(8,128)(2,1)S(1)} %bitcast.17), custom_call_target="tpu_custom_call" | custom-call | tf_op jit(solution)/shard_map/pallas_call | solution.py:382
  52.2 0.7 %copy.14 = bf16[96,1,8,128]{3,2,1,0:T(8,128)(2,1)} copy(bf16[96,1,8,128]{3,2,1,0:T(8,128)(2,1)S(1)} %bitcast.15) | data formatting | bytes 393216
  52.9 0.7 %copy.15 = bf16[96,1,8,128]{3,2,1,0:T(8,128)(2,1)} copy(bf16[96,1,8,128]{3,2,1,0:T(8,128)(2,1)S(1)} %bitcast.14) | data formatting | bytes 393216
  53.6 1.1 %copy.16 = f32[9,96,384]{2,1,0:T(8,128)} copy(f32[9,96,384]{2,1,0:T(8,128)S(1)} %bitcast.12) | data formatting | bytes 2654208
  54.6 0.5 copy.17
Async XLA Ops:
  0.6 1.1 %copy-start = (bf16[9,96,384]{2,1,0:T(8,128)(2,1)S(1)}, bf16[9,96,384]{2,1,0:T(8,128)(2,1)}, u32[]{:S(2)}) copy-start(bf16[9,96,384]{2,1,0:T(8,128)(2,1)} %param.5) | copy-start | bytes 1990660
  1.7 0.9 %copy-start.1 = (bf16[96,1,8,128]{3,2,1,0:T(8,128)(2,1)S(1)}, bf16[96,1,8,128]{3,2,1,0:T(8,128)(2,1)}, u32[]{:S(2)}) copy-start(bf16[96,1,8,128]{3,2,1,0:T(8,128)(2,1)} %param.4) | copy-start | bytes 589828
  2.6 0.9 %copy-start.2 = (bf16[96,1,8,128]{3,2,1,0:T(8,128)(2,1)S(1)}, bf16[96,1,8,128]{3,2,1,0:T(8,128)(2,1)}, u32[]{:S(2)}) copy-start(bf16[96,1,8,128]{3,2,1,0:T(8,128)(2,1)} %param.7) | copy-start | bytes 589828
  3.6 0.7 %copy-start.3 = (f32[96]{0:T(128)S(1)}, f32[96]{0:T(128)}, u32[]{:S(2)}) copy-start(f32[96]{0:T(128)} %param.6) | copy-start | bytes 1156

commit v2 on v1

v2 whole, which is shorter than its diff:
```python
import functools
import math

import jax
import jax.numpy as jnp
from jax import lax
from jax.experimental import pallas as pl
from jax.experimental.pallas import tpu as pltpu
from jax.sharding import PartitionSpec as P


def with_halo(shard, sides, width):
    for axis, dim in sides:
        devices, length = (lax.axis_size(axis), shard.shape[dim])
        up = [(i, (i + 1) % devices) for i in range(devices - 1)]
        down = [(j, i) for i, j in up]
        last = lax.slice_in_dim(shard, length - width, length, axis=dim)
        leading = lax.slice_in_dim(shard, 0, width, axis=dim)
        before = lax.ppermute(last, axis, up)
        after = lax.ppermute(leading, axis, down)
        shard = jnp.concatenate([before, shard, after], axis=dim)
    return shard


def tap_offsets():
    return [(a, b) for a in (-1, 0, 1) for b in (-1, 0, 1)]


def pad_columns(block):
    return jnp.pad(block, ((0, 0), (0, 0), (0, 0), (2, 2)))


def window_of(padded, a, b, rows, wide):
    count = padded.shape[0]
    return padded[:, :, 2 + 2 * a : 2 + 2 * a + rows, 2 + 2 * b : 2 + 2 * b + wide].reshape(
        count, -1
    )


def contract_lead(left, right):
    return lax.dot_general(
        left, right, (((0,), (0,)), ((), ())), preferred_element_type=jnp.float32
    )


def contract_last(left, right):
    return lax.dot_general(
        left, right, (((1,), (1,)), ((), ())), preferred_element_type=jnp.float32
    )


def activate(pre, cot_flat):
    output = jax.nn.gelu(pre, approximate=True).astype(jnp.bfloat16)
    _, pull = jax.vjp(lambda v: jax.nn.gelu(v, approximate=True), pre)
    grad_pre = pull(cot_flat.astype(jnp.float32))[0].astype(jnp.bfloat16)
    return (output, grad_pre)


def per_device(inputs, weight, bias, cotangent):
    chans, depth, rows, wide = inputs.shape
    out_local = bias.shape[0]
    cells = depth * rows * wide
    x_rim = with_halo(inputs, (("xy", 2),), 2)
    x_pad = pad_columns(x_rim)
    total = jnp.zeros((lax.axis_size("ch") * out_local, cells), jnp.float32)
    for t, (term_a, term_b) in enumerate(tap_offsets()):
        total = total + contract_lead(weight[t], window_of(x_pad, term_a, term_b, rows, wide))
    pre = lax.psum_scatter(
        total.reshape(lax.axis_size("ch") * out_local, depth, rows, wide),
        "ch",
        scatter_dimension=0,
        tiled=True,
    ).reshape(out_local, cells)
    pre = pre + bias[:, None]
    out_flat, grad_pre = activate(pre, cotangent.reshape(out_local, -1))
    g_rim = with_halo(grad_pre.reshape(out_local, depth, rows, wide), (("xy", 2),), 2)
    windows = [window_of(x_pad, a, b, rows, wide) for a, b in tap_offsets()]
    piece = lax.all_gather(g_rim, "ch", axis=0, tiled=True)
    grad_acc = jnp.zeros((chans, cells), jnp.float32)
    count = piece.shape[0]
    padded = pad_columns(piece)
    center = piece[:, :, 2 : 2 + rows, :].reshape(count, -1)
    pieces_w = []
    for t, (a, b) in enumerate(tap_offsets()):
        w_block = weight[t]
        g_win = padded[:, :, 2 - 2 * a : 2 - 2 * a + rows, 2 - 2 * b : 2 - 2 * b + wide].reshape(
            count, -1
        )
        grad_acc = grad_acc + jnp.dot(w_block, g_win, preferred_element_type=jnp.float32)
        pieces_w.append(contract_last(windows[t], center))
    fresh = jnp.stack(pieces_w, 0)
    grad_acc, grad_w = (grad_acc, fresh)
    grad_b = jnp.sum(grad_pre.astype(jnp.float32), axis=1)
    output = out_flat.reshape(out_local, depth, rows, wide)
    grad_x = grad_acc.astype(jnp.bfloat16).reshape(chans, depth, rows, wide)
    grad_w, grad_b = lax.psum((grad_w, grad_b), "xy")
    return (output, grad_x, grad_w, grad_b)


F32 = jnp.float32
BF16 = jnp.bfloat16
SLOPE = math.sqrt(2.0 / math.pi)
THIRDS = 3


def fused_kernel(
    nch, nxy, x_hbm, w_hbm, b_hbm, cot_hbm,
    out_ref, gx_ref, gw_ref, gb_ref,
    x_in, w_ref, b_ref, cot_in,
    xrow, crow, orow, x2d, xim, wp, pm, pf, pb, prv, g2d, sacc,
    gwf, csend, crecv, zsend, zrecv, fin,
    ls, xs, xr, ps, pr, gs, gr, hs, hr, cs, cr, zs, zr, as_, ar, fs, fr,
):
    cl, rows, wide = x_in.shape
    co = w_ref.shape[1]
    cells = rows * wide
    rim = 2 * wide
    kc = 9 * cl
    sub = cl // THIRDS
    tri = nch * sub
    me = lax.axis_index("ch")
    xy = lax.axis_index("xy")
    core = lax.rem(xy, 2)
    nz = nxy // 2
    z = xy // 2
    hrows = crecv.shape[1]
    shard = hrows // nz
    part = kc // 2
    partner = xy + 1 - 2 * core
    up = xy > 0
    down = xy < nxy - 1

    def peer(d):
        return lax.rem(me + d, nch)

    def zpeer(d):
        return lax.rem(z + d, nz) * 2 + core

    def remote(src, dst, ssem, rsem, **where):
        return pltpu.make_async_remote_copy(
            src_ref=src, dst_ref=dst, send_sem=ssem, recv_sem=rsem,
            device_id=where, device_id_type=pl.DeviceIdType.MESH,
        )

    loads = [
        pltpu.make_async_copy(src, dst, ls.at[i])
        for i, (src, dst) in enumerate(((x_hbm, x_in), (w_hbm, w_ref), (cot_hbm, cot_in), (b_hbm, b_ref)))
    ]
    for c in loads:
        c.start()

    barrier = pltpu.get_barrier_semaphore()
    for d in range(1, nch):
        pl.semaphore_signal(barrier, inc=1, device_id={"ch": peer(d)}, device_id_type=pl.DeviceIdType.MESH)
    for d in range(1, nxy):
        pl.semaphore_signal(
            barrier, inc=1, device_id={"xy": lax.rem(xy + d, nxy)}, device_id_type=pl.DeviceIdType.MESH
        )

    loads[0].wait()
    xrow[...] = x_in[...].astype(F32).reshape(cl * rows, wide)
    for r in range(rows):
        x2d[:, rim + r * wide : rim + (r + 1) * wide] = xrow[pl.ds(r, cl, stride=rows), :].astype(BF16)

    col = lax.broadcasted_iota(jnp.int32, (co, co), 1)
    rest = lax.rem(col, tri)
    target = lax.div(rest, sub) * cl + lax.div(col, tri) * sub + lax.rem(rest, sub)
    pm[...] = (lax.broadcasted_iota(jnp.int32, (co, co), 0) == target).astype(F32).astype(BF16)

    pl.semaphore_wait(barrier, nch - 1 + nxy - 1)

    to_up = remote(
        x2d.at[:, pl.ds(rim, rim)], x2d.at[:, pl.ds(rim + cells, rim)],
        xs.at[0], xr.at[0], xy=jnp.maximum(xy - 1, 0),
    )
    to_down = remote(
        x2d.at[:, pl.ds(cells, rim)], x2d.at[:, pl.ds(0, rim)],
        xs.at[1], xr.at[1], xy=jnp.minimum(xy + 1, nxy - 1),
    )
    pl.when(up)(to_up.start)
    pl.when(down)(to_down.start)

    loads[1].wait()
    wp[...] = jnp.dot(w_ref[...], pm[...], preferred_element_type=F32).astype(BF16)

    lane = lax.broadcasted_iota(jnp.int32, (cl, wide), 1)

    def spread(src_row):
        v = x2d[:, src_row * wide : (src_row + 1) * wide]
        vf = v.astype(F32)
        minus = jnp.where(lane >= 2, pltpu.roll(vf, 2, 1), 0.0).astype(BF16)
        plus = jnp.where(lane < wide - 2, pltpu.roll(vf, wide - 2, 1), 0.0).astype(BF16)
        for a in (-1, 0, 1):
            r = src_row - 2 - 2 * a
            if 0 <= r < rows:
                for b, val in ((-1, minus), (0, v), (1, plus)):
                    t = 3 * (a + 1) + b + 1
                    xim[t * cl : (t + 1) * cl, r * wide : (r + 1) * wide] = val

    for src_row in range(2, rows + 2):
        spread(src_row)
    xim[kc:, :] = jnp.ones((xim.shape[0] - kc, cells), BF16)

    def edge_zero(cond, ref, start):
        @pl.when(jnp.logical_not(cond))
        def _():
            ref[:, start : start + rim] = jnp.zeros((ref.shape[0], rim), BF16)

    edge_zero(up, x2d, 0)
    edge_zero(down, x2d, rim + cells)
    edge_zero(up, g2d, 0)
    edge_zero(down, g2d, rim + cells)

    loads[2].wait()
    loads[3].wait()
    crow[...] = cot_in[...].astype(F32).reshape(cl * rows, wide)
    eye = lax.broadcasted_iota(jnp.int32, (cl, cl), 0) == lax.broadcasted_iota(jnp.int32, (cl, cl), 1)
    bias = jnp.sum(jnp.where(eye, jnp.broadcast_to(b_ref[...], (cl, cl)), 0.0), axis=1, keepdims=True)

    pl.when(up)(to_down.wait_recv)
    pl.when(down)(to_up.wait_recv)
    for src_row in (0, 1, rows + 2, rows + 3):
        spread(src_row)

    def block(q, j):
        return pl.ds(pl.multiple_of(q * tri + j * sub, 16), sub)

    sends = []
    psends = {}
    gsends = {}
    hsends = {}
    ccopies = {}
    zcopies = {}
    acopies = {}
    fcopies = {}

    def forward(q):
        rs = slice(q * tri, (q + 1) * tri)
        val = contract_lead(wp[:, rs], xim[:kc, :])
        pf[rs, :] = val
        pb[rs, :] = val.astype(BF16)

    def send_partial(q):
        for d in range(1, nch):
            k = q * (nch - 1) + d - 1
            c = remote(pb.at[block(q, peer(d)), :], prv.at[k], ps.at[k], pr.at[k], ch=peer(d))
            c.start()
            psends[(q, d)] = c

    def activation(q):
        for d in range(1, nch):
            psends[(q, d)].wait_recv()
        if q == 1:
            send_partial(2)
        mine = block(q, me)
        for r in range(rows):
            rc = pl.ds(r * wide, wide)
            v = pf[mine, rc] + bias[q * sub : (q + 1) * sub]
            for d in range(1, nch):
                v = v + prv[q * (nch - 1) + d - 1, :, rc].astype(F32)
            sq = v * v
            th = jnp.tanh(SLOPE * (v + 0.044715 * (sq * v)))
            hp = 0.5 * (1.0 + th)
            spot = pl.ds(q * sub * rows + r, sub, stride=rows)
            orow[spot, :] = v * hp
            slope = hp + 0.5 * v * (1.0 - th * th) * (SLOPE * (1.0 + 3.0 * 0.044715 * sq))
            g2d[mine, pl.ds(rim + r * wide, wide)] = (crow[spot, :] * slope).astype(BF16)
        blk = g2d.at[mine, pl.ds(rim, cells)]
        for d in range(1, nch):
            k = q * (nch - 1) + d - 1
            c = remote(blk, blk, gs.at[k], gr.at[k], ch=peer(d))
            c.start()
            gsends[(q, d)] = c
            sends.append(c)

    def kernel_grad(q):
        for d in range(1, nch):
            gsends[(q, d)].wait_recv()
        rs = pl.ds(q * tri, tri)
        c = remote(
            g2d.at[rs, pl.ds(rim, rim)], g2d.at[rs, pl.ds(rim + cells, rim)],
            hs.at[2 * q], hr.at[2 * q], xy=jnp.maximum(xy - 1, 0),
        )
        pl.when(up)(c.start)
        hsends[(q, 0)] = c
        c = remote(
            g2d.at[rs, pl.ds(cells, rim)], g2d.at[rs, pl.ds(0, rim)],
            hs.at[2 * q + 1], hr.at[2 * q + 1], xy=jnp.minimum(xy + 1, nxy - 1),
        )
        pl.when(down)(c.start)
        hsends[(q, 1)] = c
        gwf[q] = contract_last(xim[...], g2d[rs, rim : rim + cells])
        theirs = pl.ds(pl.multiple_of((1 - core) * part, 16), hrows)
        csend[q] = gwf[q, theirs, :].astype(BF16)
        c = remote(csend.at[q], crecv.at[q], cs.at[q], cr.at[q], xy=partner)
        c.start()
        ccopies[q] = c
        sends.append(c)

    def scatter_z(q):
        ccopies[q].wait_recv()
        mine = pl.ds(pl.multiple_of(core * part, 16), hrows)
        val = gwf[q, mine, :] + crecv[q].astype(F32)
        gwf[q, mine, :] = val
        zsend[q] = val.astype(BF16)
        for d in range(1, nz):
            k = q * (nz - 1) + d - 1
            at = pl.ds(pl.multiple_of(lax.rem(z + d, nz) * shard, 16), shard)
            c = remote(zsend.at[q, at, :], zrecv.at[k], zs.at[k], zr.at[k], xy=zpeer(d))
            c.start()
            zcopies[(q, d)] = c
            sends.append(c)

    def gather_z(q):
        total = gwf[q, pl.ds(pl.multiple_of(core * part + z * shard, 16), shard), :]
        for d in range(1, nz):
            zcopies[(q, d)].wait_recv()
            total = total + zrecv[q * (nz - 1) + d - 1].astype(F32)
        at = pl.ds(pl.multiple_of(z * shard, 16), shard)
        fin[q, core, at, :] = total.astype(BF16)
        blk = fin.at[q, core, at, :]
        for d in range(1, nz):
            k = q * (nz - 1) + d - 1
            c = remote(blk, blk, as_.at[k], ar.at[k], xy=zpeer(d))
            c.start()
            acopies[(q, d)] = c
            sends.append(c)
        c = remote(blk, blk, fs.at[q * nz], fr.at[q * nz], xy=partner)
        c.start()
        fcopies[(q, 0)] = c
        sends.append(c)

    def gather_core(q):
        for d in range(1, nz):
            acopies[(q, d)].wait_recv()
            at = pl.ds(pl.multiple_of(lax.rem(z - d + nz, nz) * shard, 16), shard)
            blk = fin.at[q, core, at, :]
            c = remote(blk, blk, fs.at[q * nz + d], fr.at[q * nz + d], xy=partner)
            c.start()
            fcopies[(q, d)] = c
            sends.append(c)

    def finish(q):
        for d in range(nz):
            fcopies[(q, d)].wait_recv()
        back = pm[:, q * tri : (q + 1) * tri]
        for h in range(2):
            val = contract_last(fin[q, h, :part, :], back)
            if q == 0:
                gw_ref[h * part : (h + 1) * part, :] = val
            else:
                gw_ref[h * part : (h + 1) * part, :] += val
        i = lax.broadcasted_iota(jnp.int32, (tri, wide), 0) - me * sub
        j = lax.broadcasted_iota(jnp.int32, (tri, wide), 1) - q * sub
        pick = ((i == j) & (j >= 0) & (j < sub)).astype(F32).astype(BF16)
        gb = jnp.dot(fin[q, 1, part:, :], pick, preferred_element_type=F32)[0:1, :cl]
        if q == 0:
            gb_ref[...] = gb
        else:
            gb_ref[...] += gb

    pairs = rows // 2
    group = 3 * cl
    seen = set()

    def gi_chunk(k):
        val = jnp.dot(wp[...], g2d[:, k * rim : (k + 1) * rim], preferred_element_type=F32)
        for a in (-1, 0, 1):
            p = k - 1 + a
            if 0 <= p < pairs:
                piece = val[(a + 1) * group : (a + 2) * group]
                if p in seen:
                    sacc[:, p * rim : (p + 1) * rim] += piece
                else:
                    seen.add(p)
                    sacc[:, p * rim : (p + 1) * rim] = piece

    forward(0)
    send_partial(0)
    forward(1)
    forward(2)
    for d in range(1, nch):
        psends[(0, d)].wait_send()
    send_partial(1)
    activation(0)
    activation(1)
    for d in range(1, nch):
        psends[(1, d)].wait_send()
    kernel_grad(0)
    scatter_z(0)
    activation(2)
    for d in range(1, nch):
        psends[(2, d)].wait_send()
    out_ref[...] = orow[...].reshape(cl, rows, wide).astype(BF16)
    gather_z(0)
    kernel_grad(1)
    scatter_z(1)
    gather_core(0)
    kernel_grad(2)
    scatter_z(2)
    finish(0)
    gather_z(1)
    for q in range(THIRDS):
        pl.when(up)(hsends[(q, 1)].wait_recv)
        pl.when(down)(hsends[(q, 0)].wait_recv)
    for k in range(pairs + 2):
        gi_chunk(k)
    gather_core(1)
    gather_z(2)
    for r in range(rows):
        rc = slice(r * wide, (r + 1) * wide)
        v = sacc[cl : 2 * cl, rc]
        v = v + jnp.where(lane < wide - 2, pltpu.roll(sacc[:cl, rc], wide - 2, 1), 0.0)
        v = v + jnp.where(lane >= 2, pltpu.roll(sacc[2 * cl :, rc], 2, 1), 0.0)
        xrow[pl.ds(r, cl, stride=rows), :] = v
    gx_ref[...] = xrow[...].reshape(cl, rows, wide).astype(BF16)
    finish(1)
    gather_core(2)
    finish(2)

    pl.when(up)(to_up.wait_send)
    pl.when(down)(to_down.wait_send)
    for q in range(THIRDS):
        pl.when(up)(hsends[(q, 0)].wait_send)
        pl.when(down)(hsends[(q, 1)].wait_send)
    for c in sends:
        c.wait_send()


def fits(chans, depth, rows, wide, co, nch, nxy):
    part = 9 * chans // 2
    return (
        depth == 1
        and rows % 4 == 0
        and wide == 128
        and chans % (32 * THIRDS) == 0
        and chans <= wide
        and co == nch * chans
        and (nch * chans) % (THIRDS * 128) == 0
        and nxy % 2 == 0
        and (part + 16) % (16 * (nxy // 2)) == 0
    )


def layer(inputs, weight, bias, cotangent):
    chans, depth, rows, wide = inputs.shape
    nch, nxy = lax.axis_size("ch"), lax.axis_size("xy")
    co = weight.shape[2]
    if not fits(chans, depth, rows, wide, co, nch, nxy):
        return per_device(inputs, weight, bias, cotangent)
    cells = rows * wide
    kc = 9 * chans
    nz = nxy // 2
    hrows = kc // 2 + 16
    sub = chans // THIRDS
    tri = nch * sub
    dma = pltpu.SemaphoreType.DMA
    vmem = pltpu.VMEM
    sems = (
        [4, 2, 2]
        + [THIRDS * (nch - 1)] * 4
        + [2 * THIRDS] * 2
        + [THIRDS] * 2
        + [THIRDS * (nz - 1)] * 4
        + [THIRDS * nz] * 2
    )
    out, gx, gw, gb = pl.pallas_call(
        functools.partial(fused_kernel, nch, nxy),
        out_shape=(
            jax.ShapeDtypeStruct((chans, rows, wide), BF16),
            jax.ShapeDtypeStruct((chans, rows, wide), BF16),
            jax.ShapeDtypeStruct((kc, co), F32),
            jax.ShapeDtypeStruct((1, chans), F32),
        ),
        in_specs=[pl.BlockSpec(memory_space=pltpu.HBM)] * 4,
        out_specs=[pl.BlockSpec(memory_space=vmem)] * 4,
        scratch_shapes=[
            vmem((chans, rows, wide), BF16),
            vmem((kc, co), BF16),
            vmem((1, chans), F32),
            vmem((chans, rows, wide), BF16),
            vmem((chans * rows, wide), F32),
            vmem((chans * rows, wide), F32),
            vmem((chans * rows, wide), F32),
            vmem((chans, cells + 4 * wide), BF16),
            vmem((kc + 16, cells), BF16),
            vmem((kc, co), BF16),
            vmem((co, co), BF16),
            vmem((co, cells), F32),
            vmem((co, cells), BF16),
            vmem((THIRDS * (nch - 1), sub, cells), BF16),
            vmem((co, cells + 4 * wide), BF16),
            vmem((3 * chans, cells), F32),
            vmem((THIRDS, kc + 16, tri), F32),
            vmem((THIRDS, hrows, tri), BF16),
            vmem((THIRDS, hrows, tri), BF16),
            vmem((THIRDS, hrows, tri), BF16),
            vmem((THIRDS * (nz - 1), hrows // nz, tri), BF16),
            vmem((THIRDS, 2, hrows, tri), BF16),
        ]
        + [dma((n,)) for n in sems],
        compiler_params=pltpu.CompilerParams(
            collective_id=0, has_side_effects=True, vmem_limit_bytes=60 * 1024 * 1024
        ),
    )(
        inputs.reshape(chans, rows, wide),
        weight.reshape(kc, co),
        bias.reshape(1, chans),
        cotangent.reshape(chans, rows, wide),
    )
    return (
        out.reshape(chans, depth, rows, wide),
        gx.reshape(chans, depth, rows, wide),
        gw.reshape(9, chans, co),
        gb.reshape(chans),
    )


def solution(mesh):
    placed = (P("ch", None, "xy", None), P(None, "ch", None), P("ch"), P("ch", None, "xy", None))
    return jax.shard_map(
        layer,
        mesh=mesh,
        in_specs=placed,
        out_specs=(
            P("ch", None, "xy", None),
            P("ch", None, "xy", None),
            P(None, "ch", None),
            P("ch"),
        ),
        check_vma=False,
    )
```

time: 56 us -> 54 us (0.964)
  Pallas kernels: 48 us -> 46.3 us
    pallas_call x1, Pallas kernels: 48 us -> 46.3 us  [layer(): pl.pallas_call(functools.partial(fused_kernel, nch, nxy), out_shape=(jax....]
    unnamed x12 -> x6, local copies, waits for them, and re-layouts: 6.52 us -> 6.22 us
where the time goes in v2:
time: 54 us; the launch traced here: 53.2 us
  Pallas kernels  46.3 us (86%)
  local copies, waits for them, and re-layouts  6.22 us (12%)
  between operations  0.64 us (1%)
    pallas_call x1, Pallas kernels, layer(): pl.pallas_call(functools.partial(fused_kernel, nch, nxy), out_shape=(jax....  46.3 us
    unnamed x6, local copies, waits for them, and re-layouts  6.22 us

profile of v2, /device:TPU:0, one launch (start us, length us, event | category | flops | bytes accessed | tf_op | source)
XLA Modules:
  0.0 53.2 jit_solution(17507606491179171246)
XLA Ops:
  0.6 46.3 %shard_map.75 = (bf16[96,8,128]{2,1,0:T(8,128)(2,1)}, bf16[96,8,128]{2,1,0:T(8,128)(2,1)}, f32[864,384]{1,0:T(8,128)}, f32[1,96]{1,0:T(1,128)}) custom-call(bf16[96,8,128]{2,1,0:T(8,128)(2,1)} %bitcast.16, bf16[864,384]{1,0:T(8,128)(2,1)} %bitcast.13, f32[1,96]{1,0:T(1,128)} %bitcast.18, bf16[96,8,128]{2,1,0:T(8,128)(2,1)} %bitcast.17), custom_call_target="tpu_custom_call" | custom-call | tf_op jit(solution)/shard_map/pallas_call | solution.py:467
  47.0 1.6 %copy.14 = bf16[96,1,8,128]{3,2,1,0:T(8,128)(2,1)} copy(bf16[96,1,8,128]{3,2,1,0:T(8,128)(2,1)} %bitcast.15) | data formatting | bytes 393216
  48.6 1.6 %copy.15 = bf16[96,1,8,128]{3,2,1,0:T(8,128)(2,1)} copy(bf16[96,1,8,128]{3,2,1,0:T(8,128)(2,1)} %bitcast.14) | data formatting | bytes 393216
  50.2 0.0 copy-start
  50.2 2.5 %copy.16 = f32[9,96,384]{2,1,0:T(8,128)} copy(f32[9,96,384]{2,1,0:T(8,128)} %bitcast.12) | data formatting | bytes 2654208
  52.7 0.0 copy-done
  52.7 0.5 copy.17
Async XLA Ops:
  50.2 2.5 %copy-start = (f32[1,96]{1,0:T(1,128)S(1)}, f32[1,96]{1,0:T(1,128)}, u32[]{:S(2)}) copy-start(f32[1,96]{1,0:T(1,128)} %get-tuple-element.11) | copy-start | bytes 1156
